TPU v7x, 512 devices: a whole 4x4x16 slice. The times are simulated.
512 devices in a mesh: band: 64 (over y_hi, z, core), helper: 8 (over y_lo, x).
Axes of the slice: x: 4, y: 4 (y_hi: 2, y_lo: 2; y = y_hi * 2 + y_lo), z: 16, core: 2. Of those that a mesh axis runs over, the one named last changes fastest.
Arguments:
- node_latent: bfloat16 [32768, 256], P(('band', 'helper')), may hold values from -6 to 6
- edge_latent: bfloat16 [524288, 256], P(('band', 'helper')), may hold values from -6 to 6
- grad_out_node: bfloat16 [32768, 256], P(('band', 'helper')), may hold values from -6 to 6
- grad_out_edge: bfloat16 [524288, 256], P(('band', 'helper')), may hold values from -6 to 6
- senders: int32 [524288], P(('band', 'helper')), may hold values from 0 to 767
- receivers: int32 [524288], P(('band', 'helper')), may hold values from 0 to 511, as said below
- band_edges: int32 [64], replicated, may hold values from 8 to 64, as said below
- halo_list: int32 [64, 128], P('band'), may hold values from 0 to 511, as said below
- sea_mask: int32 [32768], P(('band', 'helper')), may hold values 0 or 1
- edge_w1: bfloat16 [768, 256], replicated, may hold values from -0.21875 to 0.21875
- edge_b1: float32 [256], replicated, may hold values from -3 to 3
- edge_w2: bfloat16 [256, 256], replicated, may hold values from -0.375 to 0.375
- edge_b2: float32 [256], replicated, may hold values from -3 to 3
- node_w1: bfloat16 [512, 256], replicated, may hold values from -0.25 to 0.25
- node_b1: float32 [256], replicated, may hold values from -3 to 3
- node_w2: bfloat16 [256, 256], replicated, may hold values from -0.375 to 0.375
- node_b2: float32 [256], replicated, may hold values from -3 to 3
Outputs:
- grad_node: float32 [32768, 256], P(('band', 'helper'))
- grad_edge: bfloat16 [524288, 256], P(('band', 'helper'))
- grad_edge_w1: float32 [768, 256], replicated
- grad_edge_b1: float32 [256], replicated
- grad_edge_w2: float32 [256, 256], replicated
- grad_edge_b2: float32 [256], replicated
- grad_node_w1: float32 [512, 256], replicated
- grad_node_b1: float32 [256], replicated
- grad_node_w2: float32 [256, 256], replicated
- grad_node_b2: float32 [256], replicated
Inputs may be any that keep to these rules, and one draw needn't show every extreme that they name: In every aligned block of 128 edge rows, all receivers lie in one aligned tile of 64 nodes. `band_edges`: A quarter of the bands, consecutive along the cycle, hold 64 live blocks; every other band holds between 8 and 24. `halo_list`: the 128 entries of a band are distinct.
All inputs are finite; a program needn't handle non-finite values. No bound on the sum of `sea_mask` on one device may be relied on, other than what follows from the above.
Results may differ from a plain program's by a relative error of at most 0.01.
Values may be sent and summed in bfloat16 or wider, within the bound.
A program may use at most 64 MiB of HBM per device.

v0:
```python
import math

import jax
import jax.numpy as jnp
from jax import lax
from jax.sharding import PartitionSpec as P

EB = 128
RTILE = 64


norm_eps = 1e-05


def passed_along(array, axis, by):
    count = lax.axis_size(axis)
    return lax.ppermute(array, axis, [(i, (i + by) % count) for i in range(count)])


def layer_norm(pre_act):
    row_mean = jnp.mean(pre_act, axis=-1, keepdims=True)
    centre = pre_act - row_mean
    inv_dev = lax.rsqrt(jnp.mean(centre * centre, axis=-1, keepdims=True) + norm_eps)
    return (centre * inv_dev, inv_dev)


def norm_back(grad_in, normed, inv_dev):
    return inv_dev * (
        grad_in
        - jnp.mean(grad_in, axis=-1, keepdims=True)
        - normed * jnp.mean(grad_in * normed, axis=-1, keepdims=True)
    )


def silu_slope(pre_act):
    sigmoid_v = jax.nn.sigmoid(pre_act)
    return sigmoid_v * (1.0 + pre_act * (1.0 - sigmoid_v))


def dot_left_t(left_op, right_op):
    return lax.dot_general(
        left_op, right_op, (((0,), (0,)), ((), ())), preferred_element_type=jnp.float32
    )


def dot_right_t(left_op, right_op):
    return lax.dot_general(
        left_op, right_op, (((1,), (1,)), ((), ())), preferred_element_type=jnp.float32
    )


def mlp_forward(inputs, w_first, b_first, w_second, b_second):
    pre_act = jnp.dot(inputs, w_first, preferred_element_type=jnp.float32) + b_first
    hidden = jax.nn.silu(pre_act).astype(jnp.bfloat16)
    normed, inv_dev = layer_norm(
        jnp.dot(hidden, w_second, preferred_element_type=jnp.float32) + b_second
    )
    return (pre_act, hidden, normed, inv_dev)


def mlp_back_parts(inputs, w_second, pre_act, hidden, normed, inv_dev, grad_out):
    grad_second = norm_back(grad_out, normed, inv_dev)
    second_b = grad_second.astype(jnp.bfloat16)
    gw_second = dot_left_t(hidden, second_b)
    gb_second = jnp.sum(grad_second, axis=0)
    grad_first = dot_right_t(second_b, w_second) * silu_slope(pre_act)
    first_b = grad_first.astype(jnp.bfloat16)
    gw_first = dot_left_t(inputs, first_b)
    gb_first = jnp.sum(grad_first, axis=0)
    return (first_b, gw_first, gb_first, gw_second, gb_second)


def mlp_backward(inputs, w_first, w_second, pre_act, hidden, normed, inv_dev, grad_out):
    parts = mlp_back_parts(inputs, w_second, pre_act, hidden, normed, inv_dev, grad_out)
    return (dot_right_t(parts[0], w_first),) + parts[1:]


def tile_sum(running, recv_ids, values):
    tile_base = recv_ids[0] // RTILE * RTILE
    local_ids = recv_ids - tile_base
    onehot = local_ids[:, None] == jnp.arange(RTILE, dtype=jnp.int32)[None, :]
    if values.dtype == jnp.bfloat16:
        tile_part = dot_left_t(onehot.astype(jnp.bfloat16), values)
    else:
        tile_part = lax.dot_general(
            onehot.astype(jnp.float32),
            values,
            (((0,), (0,)), ((), ())),
            precision=lax.Precision.HIGHEST,
            preferred_element_type=jnp.float32,
        )
    current = lax.dynamic_slice_in_dim(running, tile_base, RTILE, 0)
    return lax.dynamic_update_slice_in_dim(running, current + tile_part, tile_base, 0)


def on_device(
    node_latent,
    edge_latent,
    grad_out_node,
    grad_out_edge,
    senders,
    receivers,
    band_edges,
    halo_list,
    sea_mask,
    edge_w1,
    edge_b1,
    edge_w2,
    edge_b2,
    node_w1,
    node_b1,
    node_w2,
    node_b2,
):
    features = node_latent.shape[1]
    helpers = lax.axis_size("helper")
    band_count = lax.axis_size("band")
    helper_idx = lax.axis_index("helper")
    band_idx = lax.axis_index("band")
    node_dev = node_latent.shape[0]
    band_size = node_dev * helpers
    halo_size = halo_list.shape[1]
    edge_block = EB
    slot_count = edge_latent.shape[0] // edge_block
    edge_blocks = edge_latent.reshape(slot_count, edge_block, features)
    grad_blocks = grad_out_edge.reshape(slot_count, edge_block, features)
    send_blocks = senders.reshape(slot_count, edge_block)
    recv_blocks = receivers.reshape(slot_count, edge_block)
    halo_ids = halo_list[0]
    band_rows = lax.all_gather(node_latent, "helper", axis=0, tiled=True)
    outgoing = band_rows[halo_ids]
    from_prev = passed_along(outgoing, "band", 1)
    from_next = passed_along(outgoing, "band", -1)
    lookup = jnp.concatenate([band_rows, from_prev, from_next], axis=0)
    live_count = band_edges[band_idx]
    own_live = jnp.clip((live_count - helper_idx + helpers - 1) // helpers, 0, slot_count)

    def inputs_of(slot_id):
        return jnp.concatenate(
            [lookup[send_blocks[slot_id]], band_rows[recv_blocks[slot_id]], edge_blocks[slot_id]],
            axis=1,
        )

    def message_of(inputs):
        normed = mlp_forward(inputs, edge_w1, edge_b1, edge_w2, edge_b2)[2]
        return normed.astype(jnp.bfloat16)

    def add_own(slot_id, agg_rows):
        return tile_sum(agg_rows, recv_blocks[slot_id], message_of(inputs_of(slot_id)))

    agg_start = jnp.zeros((band_size, features), jnp.float32)
    agg_rows = lax.fori_loop(0, own_live, add_own, agg_start)
    agg_own = lax.psum_scatter(agg_rows, "helper", scatter_dimension=0, tiled=True)
    node_in = jnp.concatenate([node_latent, agg_own.astype(jnp.bfloat16)], axis=1)
    n_pre, n_hidden, n_normed, n_inv = mlp_forward(node_in, node_w1, node_b1, node_w2, node_b2)
    node_seed = sea_mask[:, None].astype(jnp.float32) * grad_out_node.astype(jnp.float32)
    node_back = mlp_backward(node_in, node_w1, node_w2, n_pre, n_hidden, n_normed, n_inv, node_seed)
    agg_grad = node_back[0][:, features:].astype(jnp.bfloat16)
    agg_band = lax.all_gather(agg_grad, "helper", axis=0, tiled=True)

    def edge_parts(inputs, grad_edge_in, agg_rows_in):
        msg_grad = grad_edge_in.astype(jnp.float32) + agg_rows_in.astype(jnp.float32)
        pre_act, hidden, normed, inv_dev = mlp_forward(inputs, edge_w1, edge_b1, edge_w2, edge_b2)
        return mlp_back_parts(inputs, edge_w2, pre_act, hidden, normed, inv_dev, msg_grad)

    def settle(lookup_grad, edge_out, slot_id, first_b):
        grad_inputs = dot_right_t(first_b, edge_w1)
        lookup_grad = lookup_grad.at[send_blocks[slot_id]].add(grad_inputs[:, :features])
        lookup_grad = tile_sum(
            lookup_grad, recv_blocks[slot_id], grad_inputs[:, features : 2 * features]
        )
        edge_new = (
            grad_blocks[slot_id].astype(jnp.float32) + grad_inputs[:, 2 * features :]
        ).astype(jnp.bfloat16)
        return (lookup_grad, edge_out.at[slot_id].set(edge_new))

    def own_step(slot_id, loop_state):
        first_b, gw_one, gb_one, gw_two, gb_two = edge_parts(
            inputs_of(slot_id), grad_blocks[slot_id], agg_band[recv_blocks[slot_id]]
        )
        lookup_grad, edge_out = settle(loop_state[0], loop_state[1], slot_id, first_b)
        return (
            lookup_grad,
            edge_out,
            loop_state[2] + gw_one,
            loop_state[3] + gb_one,
            loop_state[4] + gw_two,
            loop_state[5] + gb_two,
        )

    start_state = (
        jnp.zeros((band_size + 2 * halo_size, features), jnp.float32),
        jnp.zeros((slot_count, edge_block, features), jnp.bfloat16),
        jnp.zeros(edge_w1.shape, jnp.float32),
        jnp.zeros((features,), jnp.float32),
        jnp.zeros(edge_w2.shape, jnp.float32),
        jnp.zeros((features,), jnp.float32),
    )
    final_state = lax.fori_loop(0, own_live, own_step, start_state)
    lookup_grad, edge_out = (final_state[0], final_state[1])
    edge_wgrads = final_state[2:]
    band_grad = lookup_grad[:band_size]
    prev_region = lookup_grad[band_size : band_size + halo_size]
    next_region = lookup_grad[band_size + halo_size :]
    from_next_band = passed_along(prev_region.astype(jnp.bfloat16), "band", -1).astype(
        prev_region.dtype
    )
    from_prev_band = passed_along(next_region.astype(jnp.bfloat16), "band", 1).astype(
        next_region.dtype
    )
    band_grad = band_grad.at[halo_ids].add(from_next_band + from_prev_band)
    node_sum = lax.psum_scatter(
        band_grad.astype(jnp.bfloat16), "helper", scatter_dimension=0, tiled=True
    ).astype(jnp.float32)
    grad_node = node_sum + grad_out_node.astype(jnp.float32) + node_back[0][:, :features]
    edge_scale = 1.0 / math.sqrt(slot_count * edge_block * helpers * band_count)
    node_scale = 1.0 / math.sqrt(node_dev * helpers * band_count)
    sums = lax.psum(
        (
            edge_wgrads[0] * edge_scale,
            edge_wgrads[1] * edge_scale,
            edge_wgrads[2] * edge_scale,
            edge_wgrads[3] * edge_scale,
            node_back[1] * node_scale,
            node_back[2] * node_scale,
            node_back[3] * node_scale,
            node_back[4] * node_scale,
        ),
        ("band", "helper"),
    )
    grad_edge = edge_out.reshape(slot_count * edge_block, features)
    return (
        grad_node,
        grad_edge,
        sums[0],
        sums[1],
        sums[2],
        sums[3],
        sums[4],
        sums[5],
        sums[6],
        sums[7],
    )


def solution(mesh):
    in_specs = (
        P(("band", "helper"), None),
        P(("band", "helper"), None),
        P(("band", "helper"), None),
        P(("band", "helper"), None),
        P(("band", "helper")),
        P(("band", "helper")),
        P(),
        P("band", None),
        P(("band", "helper")),
        P(),
        P(),
        P(),
        P(),
        P(),
        P(),
        P(),
        P(),
    )
    out_specs = (
        P(("band", "helper"), None),
        P(("band", "helper"), None),
        P(),
        P(),
        P(),
        P(),
        P(),
        P(),
        P(),
        P(),
    )
    return jax.shard_map(
        on_device, mesh=mesh, in_specs=in_specs, out_specs=out_specs, check_vma=False
    )
```

profile of v0, /device:TPU:1, one launch (start us, length us, event | category | flops | bytes accessed | tf_op | source)
XLA Modules:
  0.0 885.0 jit_solution(7241035239836565681)
XLA Ops:
  7.2 23.7 %all_gather.6 = bf16[512,256]{1,0:T(8,128)(2,1)S(1)} all-gather(bf16[64,256]{1,0:T(8,128)(2,1)} %param.23), channel_id=1, replica_groups=mesh['band'=64,'helper'=8] {'helper'}, dimensions={0}, use_global_device_ids=true | all-gather | bytes 294912 | tf_op jit(solution)/shard_map/all_gather | solution.py:130
  32.3 10.5 %collective-permute-start = (bf16[128,256]{1,0:T(8,128)(2,1)S(1)}, bf16[128,256]{1,0:T(8,128)(2,1)S(1)}, u32[]{:S(2)}, u32[]{:S(2)}) collective-permute-start(bf16[128,256]{1,0:T(8,128)(2,1)S(1)} %gather_fusion.5), channel_id=1, source_target_pairs={{0,8},{8,16},{16,24},{24,32},{32,40},{40,48},{48,56},{56,64},{64,7... | collective-permute-start | bytes 196616 | tf_op jit(solution)/shard_map/ppermute | solution.py:17
  42.8 5.3 collective-permute-start.1
  51.1 5.8 while.35
  55.1 1.1 fusion.120
  58.4 76.6 %reduce-scatter.3.cloned.1.call-done = f32[64,256]{1,0:T(8,128)} async-done(((f32[512,256]{1,0:T(8,128)}), f32[64,256]{1,0:T(8,128)}) %reduce-scatter.3.cloned.1.call-update) | async-done | bytes 65552 | tf_op jit(solution)/shard_map/reduce_scatter | solution.py:153
  140.1 22.1 %all_gather.7 = bf16[512,256]{1,0:T(8,128)(2,1)S(1)} all-gather(bf16[64,256]{1,0:T(8,128)(2,1)S(1)} %slice.106), channel_id=1, replica_groups=mesh['band'=64,'helper'=8] {'helper'}, dimensions={0}, use_global_device_ids=true | all-gather | bytes 294912 | tf_op jit(solution)/shard_map/all_gather | solution.py:159
  164.1 20.9 %while.36 = (s32[]{:T(128)}, f32[768,256]{1,0:T(8,128)}, bf16[8,128,256]{2,1,0:T(8,128)(2,1)}, f32[768,256]{1,0:T(8,128)S(1)}, f32[256]{0:T(256)S(1)}, /*index=5...) while((s32[]{:T(128)}, f32[768,256]{1,0:T(8,128)}, ...), condition=%wide.region_18.19_spmd, body=%wide.region_9.18_spmd.sunk | while | flops 229600272 | bytes 8767240 | solution.py:199
  169.0 0.9 fusion.134
  171.0 1.0 fusion.135
  172.0 1.0 fusion.136
  174.1 3.3 scatter_custom_fusion.7
  177.6 1.8 fusion.139
  181.1 2.2 fusion.140
  185.0 1.2 convert.9
  186.2 55.3 %collective-permute-start.2 = (bf16[128,256]{1,0:T(8,128)(2,1)S(1)}, bf16[128,256]{1,0:T(8,128)(2,1)S(1)}, u32[]{:S(2)}, u32[]{:S(2)}) collective-permute-start(bf16[128,256]{1,0:T(8,128)(2,1)S(1)} %get-tuple-element.514), channel_id=1, source_target_pairs={{0,504},{8,0},{16,8},{24,16},{32,24},{40,32},{48,40},{56,48},{64,5... | collective-permute-start | bytes 196616 | tf_op jit(solution)/shard_map/ppermute | solution.py:17
  241.6 3.0 collective-permute-start.3
  245.9 1.6 scatter_custom_fusion.1
  250.0 1.0 convolution_multiply_fusion.1
  251.1 1.0 broadcast_multiply_fusion.4
  253.5 207.8 %all-reduce = (f32[256]{0:T(256)}, f32[256]{0:T(256)}, f32[256]{0:T(256)}, f32[256]{0:T(256)}) all-reduce(f32[256]{0:T(256)S(1)} %broadcast_multiply_fusion.9, f32[256]{0:T(256)S(1)} %broadcast_multiply_fusion.8, f32[256]{0:T(256)S(1)} %broadcast_multiply_fusion.7, ...), channel_id=1, replica_groups=mesh['band'=64,'helper'=8] {'band','helper'}, use_global_device_ids=true, to_apply=%region_22.23 | all-reduce | flops 1024 | bytes 8192 | tf_op jit(solution)/shard_map/psum | solution.py:218
  461.3 1.4 fusion.51
  462.7 410.8 %all-reduce.4.cloned.1.call-done = (f32[768,256]{1,0:T(8,128)}, f32[256,256]{1,0:T(8,128)}, f32[512,256]{1,0:T(8,128)}, f32[256,256]{1,0:T(8,128)}) async-done(((f32[768,256]{1,0:T(8,128)}, f32[256,256]{1,0:T(8,128)}, f32[512,256]{1,0:T(8,128)}, f32[256,256]{1,0:T(8,128)}), (f32[768,256]{1,0:T(8,128)}, f32[256,256]{1,0:T(8,128)}, f32[512,256]{1,0:T(8,128)}, ...) | async-done | bytes 1835024 | tf_op jit(solution)/shard_map/psum | solution.py:218
  873.5 2.1 copy.65
  (155 shorter events, 34.8 us)
Async XLA Ops:
  7.2 128.7 %copy-start = (bf16[512,256]{1,0:T(8,128)(2,1)S(1)}, bf16[512,256]{1,0:T(8,128)(2,1)}, u32[]{:S(2)}) copy-start(bf16[512,256]{1,0:T(8,128)(2,1)} %param.36) | copy-start | bytes 786436
  7.2 23.7 %copy-start.33 = (s32[1,128]{1,0:T(1,128)S(1)}, s32[1,128]{1,0:T(1,128)}, u32[]{:S(2)}) copy-start(s32[1,128]{1,0:T(1,128)} %param.30) | copy-start | bytes 1540
  7.2 127.8 %reduce-scatter.3.cloned.1.call-start = ((), (), s32[]{:S(2)}) async-start(), calls=%async_computation.2 | async-start | bytes 589824 | tf_op jit(solution)/shard_map/reduce_scatter | solution.py:153
  32.3 17.8 %collective-permute-start = (bf16[128,256]{1,0:T(8,128)(2,1)S(1)}, bf16[128,256]{1,0:T(8,128)(2,1)S(1)}, u32[]{:S(2)}, u32[]{:S(2)}) collective-permute-start(bf16[128,256]{1,0:T(8,128)(2,1)S(1)} %gather_fusion.5), channel_id=1, source_target_pairs={{0,8},{8,16},{16,24},{24,32},{32,40},{40,48},{48,56},{56,64},{64,7... | collective-permute-start | bytes 196616 | tf_op jit(solution)/shard_map/ppermute | solution.py:17
  42.8 7.3 collective-permute-start.1
  50.1 1.0 copy-start.1
  57.7 403.5 %reduce-scatter.5.cloned.1.call-start = ((), (), s32[]{:S(2)}) async-start(), calls=%async_computation.3 | async-start | bytes 294912 | tf_op jit(solution)/shard_map/reduce_scatter | solution.py:212
  58.4 77.5 %copy-start.7 = (bf16[64,256]{1,0:T(8,128)(2,1)S(1)}, bf16[64,256]{1,0:T(8,128)(2,1)}, u32[]{:S(2)}) copy-start(bf16[64,256]{1,0:T(8,128)(2,1)} %param.23) | copy-start | bytes 98308
  58.4 77.5 %copy-start.22 = (f32[256]{0:T(256)S(1)}, f32[256]{0:T(256)}, u32[]{:S(2)}) copy-start(f32[256]{0:T(256)} %param.37) | copy-start | bytes 3076
  136.8 1.9 copy-start.14
  140.1 22.2 %copy-start.5 = (f32[64,512]{1,0:T(8,128)}, f32[64,512]{1,0:T(8,128)S(1)}, u32[]{:S(2)}) copy-start(f32[64,512]{1,0:T(8,128)S(1)} %fusion.53) | copy-start | bytes 393220
  164.1 4.6 copy-start.31
  164.2 8.9 %copy-start.27 = (bf16[256,256]{1,0:T(8,128)(2,1)}, bf16[256,256]{1,0:T(8,128)(2,1)S(1)}, u32[]{:S(2)}) copy-start(bf16[256,256]{1,0:T(8,128)(2,1)S(1)} %get-tuple-element.885) | copy-start | bytes 393220 | tf_op jit(solution)/shard_map/while
  183.3 1.0 copy-start.28
  185.0 60.3 %copy-start.2 = (f32[768,256]{1,0:T(8,128)S(1)}, f32[768,256]{1,0:T(8,128)}, u32[]{:S(2)}) copy-start(f32[768,256]{1,0:T(8,128)} %get-tuple-element.418) | copy-start | bytes 2359300
  186.2 59.1 %collective-permute-start.2 = (bf16[128,256]{1,0:T(8,128)(2,1)S(1)}, bf16[128,256]{1,0:T(8,128)(2,1)S(1)}, u32[]{:S(2)}, u32[]{:S(2)}) collective-permute-start(bf16[128,256]{1,0:T(8,128)(2,1)S(1)} %get-tuple-element.514), channel_id=1, source_target_pairs={{0,504},{8,0},{16,8},{24,16},{32,24},{40,32},{48,40},{56,48},{64,5... | collective-permute-start | bytes 196616 | tf_op jit(solution)/shard_map/ppermute | solution.py:17
  241.6 4.3 collective-permute-start.3
  248.3 1.7 copy-start.13
  248.3 625.2 %all-reduce.4.cloned.1.call-start = ((), (), s32[]{:S(2)}) async-start(), calls=%async_computation.4 | async-start | bytes 3670016 | tf_op jit(solution)/shard_map/psum | solution.py:218
  252.0 209.2 %copy-start.6 = (f32[64,512]{1,0:T(8,128)S(1)}, f32[64,512]{1,0:T(8,128)}, u32[]{:S(2)}) copy-start(f32[64,512]{1,0:T(8,128)} %copy-done.5) | copy-start | bytes 393220
  252.0 209.2 %copy-start.9 = (bf16[64,256]{1,0:T(8,128)(2,1)S(1)}, bf16[64,256]{1,0:T(8,128)(2,1)}, u32[]{:S(2)}) copy-start(bf16[64,256]{1,0:T(8,128)(2,1)} %param.25) | copy-start | bytes 98308
  873.5 2.1 copy-start.11
  875.6 1.1 copy-start.4
  876.7 1.1 copy-start.10
  (19 other events, 14.2 us)
Sparse Core Ops, SparseCore 0:
  57.8 77.1 reduce-scatter.2
  248.4 139.0 reduce-scatter.4
  393.8 479.6 all-reduce.3
where the time goes:
time: 894 us; the launch traced here: 885 us
  waiting for transfers between devices  488 us (55%)
  blocking collectives  254 us (28%)
  starting transfers between devices  74.2 us (8%)
  local copies, waits for them, and re-layouts  24.3 us (3%)
  other arithmetic  20.2 us (2%)
  between operations  14.8 us (2%)
  matrix products  9.32 us (1%)
    psum x1, waiting for transfers between devices, on_device(): lax.psum((edge_wgrads[0] * edge_scale, edge_wgrads[1] * edge_scale, edge_...  411 us
    psum x1, blocking collectives, on_device(): lax.psum((edge_wgrads[0] * edge_scale, edge_wgrads[1] * edge_scale, edge_...  208 us
    reduce_scatter x1, waiting for transfers between devices, on_device(): lax.psum_scatter(agg_rows, 'helper', scatter_dimension=0, tiled=True)  76.6 us
    ppermute x4, starting transfers between devices, passed_along(): lax.ppermute(array, axis, [(i, (i + by) % count) for i in range(count)])  74.1 us
    all_gather x1, blocking collectives, on_device(): band_rows = lax.all_gather(node_latent, 'helper', axis=0, tiled=True)  23.7 us
    all_gather x1, blocking collectives, on_device(): agg_band = lax.all_gather(agg_grad, 'helper', axis=0, tiled=True)  22.1 us
  transfers between devices with their start and end apart: 7, of which 3 were waited for; matrix products, arithmetic and copies ran while one was open for 1% of the time, Pallas kernels for 0%

commit v1 on v0

v1 whole, which is shorter than its diff:
```python
import functools
import math
from types import SimpleNamespace

import jax
import jax.numpy as jnp
from jax import lax
from jax.experimental import pallas as pl
from jax.experimental.pallas import tpu as pltpu
from jax.sharding import PartitionSpec as P

Y_HI = 2
Y_LO = 2
Z_HI = 4
Z_LO = 4
CORES = 2
EB = 128
EARLY = 3
ROWS = 256
LANES = 128
VMEM_BYTES = 56 * 1024 * 1024

norm_eps = 1e-05
F32 = jnp.float32
BF16 = jnp.bfloat16
MESH = pl.DeviceIdType.MESH


def dot(a, b):
    return jnp.dot(a, b, preferred_element_type=F32)


def dot_nt(a, b):
    return lax.dot_general(a, b, (((1,), (1,)), ((), ())), preferred_element_type=F32)


def layer_norm(pre_act):
    row_mean = jnp.mean(pre_act, axis=-1, keepdims=True)
    centre = pre_act - row_mean
    inv_dev = lax.rsqrt(jnp.mean(centre * centre, axis=-1, keepdims=True) + norm_eps)
    return centre * inv_dev, inv_dev


def norm_back(grad_in, normed, inv_dev):
    return inv_dev * (
        grad_in
        - jnp.mean(grad_in, axis=-1, keepdims=True)
        - normed * jnp.mean(grad_in * normed, axis=-1, keepdims=True)
    )


def column(row):
    n = row.shape[1]
    diag = lax.broadcasted_iota(jnp.int32, (n, n), 0) == lax.broadcasted_iota(jnp.int32, (n, n), 1)
    return jnp.sum(jnp.where(diag, row, 0.0), axis=1, keepdims=True)


def onehot_cols(col, width):
    ids = lax.broadcasted_iota(jnp.int32, (col.shape[0], width), 1).astype(F32)
    return jnp.where(ids == col, 1.0, 0.0).astype(BF16)


def onehot_rows(row, height):
    ids = lax.broadcasted_iota(jnp.int32, (height, row.shape[1]), 0).astype(F32)
    return jnp.where(ids == row, 1.0, 0.0).astype(BF16)


def at(index, size):
    return pl.ds(pl.multiple_of(index * size, size), size)


def loop(count, body):
    if count == 1:
        body(0)
        return

    def step(i, carry):
        body(i)
        return carry

    lax.fori_loop(0, count, step, 0)


class Flow:
    def __init__(self, flows, send_sem, recv_sem, sent, landed):
        self.send_sem, self.recv_sem, self.sent, self.landed = send_sem, recv_sem, sent, landed
        self.arrived = False
        flows.append(self)

    def send(self, src, dst, device):
        pltpu.make_async_remote_copy(
            src_ref=src,
            dst_ref=dst,
            send_sem=self.send_sem,
            recv_sem=self.recv_sem,
            device_id=device,
            device_id_type=MESH,
        ).start()

    def wait(self):
        self.arrived = True
        pltpu.make_async_copy(self.landed, self.landed, self.recv_sem).wait()

    def drain(self):
        if not self.arrived:
            self.wait()
        pltpu.make_async_copy(self.sent, self.sent, self.send_sem).wait()


class Local:
    def __init__(self, flows, src, dst, sem):
        self.copy = pltpu.make_async_copy(src, dst, sem)
        self.copy.start()
        self.arrived = False
        flows.append(self)

    def wait(self):
        self.arrived = True
        self.copy.wait()

    def drain(self):
        if not self.arrived:
            self.wait()


def kernel(dims, names, *refs):
    flows = []
    r = SimpleNamespace(**dict(zip(names, refs)))
    r.n = SimpleNamespace(out=r.n_out, land=r.n_land, z_lo=r.n_z_lo, z_hi=r.n_z_hi, full=r.n_full, s=r.n_s, r=r.n_r)
    r.e = SimpleNamespace(out=r.e_out, land=r.e_land, z_lo=r.e_z_lo, z_hi=r.e_z_hi, full=r.e_full, s=r.e_s, r=r.e_r)
    steps(dims, r, flows)
    for flow in flows:
        flow.drain()


def steps(dims, r, flows):
    H, E, N, HALO, L, G = dims.H, dims.E, dims.N, dims.HALO, dims.L, dims.G
    BAND = N * H
    LOOK = BAND + 2 * HALO
    ALL = LOOK + BAND
    NBLK = E // ROWS
    ZN = Z_HI * Z_LO

    band = lax.axis_index("band")
    helper = lax.axis_index("helper")
    n_band = Y_HI * ZN * CORES
    core = lax.rem(band, CORES)
    z = lax.rem(lax.div(band, CORES), ZN)
    y_hi = lax.div(band, CORES * ZN)
    z_lo = lax.rem(z, Z_LO)
    z_hi = lax.div(z, Z_LO)
    plane = y_hi * CORES + core
    me = plane * H + helper
    X = H // Y_LO
    x, y = lax.rem(helper, X), y_hi * Y_LO + lax.div(helper, X)
    KINDS = 4
    kind_own = lax.rem(x + y + 2 * core, KINDS)

    def owner(kind, j):
        to_y, to_core = lax.rem(y + j // CORES, Y_HI * Y_LO), lax.rem(core + j % CORES, CORES)
        to_x = lax.rem(kind + 2 * KINDS - to_y - 2 * to_core, KINDS)
        to_plane = lax.div(to_y, Y_LO) * CORES + to_core
        to_helper = lax.rem(to_y, Y_LO) * X + to_x
        return to_plane * H + to_helper, (to_core * KINDS + kind) * (Y_HI * Y_LO) + to_y, place(to_plane, z, to_helper)

    def place(plane_i, z_i, helper_i):
        return dict(
            band=(lax.div(plane_i, CORES) * ZN + z_i) * CORES + lax.rem(plane_i, CORES),
            helper=helper_i,
        )

    def in_group(k):
        g = lax.rem(me + k, G)
        return g, place(lax.div(g, H), z, lax.rem(g, H))

    def in_helper(k):
        return dict(band=band, helper=lax.rem(helper + k, H))

    def in_plane(k):
        return place(lax.rem(plane + k, Y_HI * CORES), z, helper)

    def in_z_lo(k):
        return place(plane, z_hi * Z_LO + lax.rem(z_lo + k, Z_LO), helper)

    def in_z_hi(k):
        return place(plane, lax.rem(z_hi + k, Z_HI) * Z_LO + z_lo, helper)

    next_band = dict(band=lax.rem(band + 1, n_band), helper=helper)
    prev_band = dict(band=lax.rem(band + n_band - 1, n_band), helper=helper)

    def flow(i, sent, landed):
        return Flow(flows, r.s_sem.at[i], r.r_sem.at[i], sent, landed)

    load_edge = Local(flows, r.edge_hbm, r.edge, r.load_sem.at[0])
    load_grad = Local(flows, r.gedge_hbm, r.gedge, r.load_sem.at[1])

    barrier = pltpu.get_barrier_semaphore()

    def greet(device):
        pl.semaphore_signal(barrier, inc=1, device_id=device, device_id_type=MESH)

    for k in range(1, G):
        greet(in_group(k)[1])
    for k in range(1, Z_LO):
        greet(in_z_lo(k))
    for k in range(1, Z_HI):
        greet(in_z_hi(k))
    greet(next_band)
    greet(prev_band)
    hot, hot_t = r.hot, r.hot_t

    def block_onehots(j):
        rows = at(j, EB)
        s_row, r_row = r.send_ids[pl.ds(j, 1), :].astype(F32), r.recv_ids[pl.ds(j, 1), :].astype(F32)
        hot[rows, :LOOK] = onehot_cols(column(s_row), LOOK)
        hot[rows, LOOK:] = onehot_cols(column(r_row), BAND)
        hot_t[:LOOK, rows] = onehot_rows(s_row, LOOK)
        hot_t[LOOK:, rows] = onehot_rows(r_row, BAND)

    loop(EARLY, block_onehots)
    pl.semaphore_wait(barrier, G - 1 + Z_LO - 1 + Z_HI - 1 + 2)

    look, proj = r.look, r.proj
    others = look.at[pl.ds(0, (H - 1) * N)]
    rows_flow = flow(0, others, others)
    for k in range(1, H):
        rows_flow.send(r.node, look.at[at(helper, N)], in_helper(k))
    look[at(helper, N), :] = r.node[...]


    loop(E // EB - EARLY, lambda j: block_onehots(j + EARLY))
    halo_row = r.halo[...].astype(F32)
    halo_t = onehot_rows(halo_row, BAND)
    r.halo_t[:, :HALO] = halo_t
    r.halo_t[:, HALO:] = halo_t
    sea = column(r.sea[...].astype(F32))

    live_blocks = r.band_edges[band]
    slot = lax.shift_right_logical(lax.broadcasted_iota(jnp.int32, (E, 1), 0), int(math.log2(EB)))
    r.live[...] = jnp.where(slot * H + helper < live_blocks, 1.0, 0.0)

    load_edge.wait()
    edge, pre = r.edge, r.pre

    def edge_part(i):
        rows = at(i, ROWS)
        block = edge[rows, :]
        pre[rows, :] = dot(block, r.ew1[2 * L :, :]) + r.eb1[...]
        r.edge_t[:, rows] = block.T

    loop(NBLK, edge_part)

    rows_flow.wait()
    r.halo_out[...] = dot(onehot_cols(column(halo_row), BAND), look[:BAND, :]).astype(BF16)
    from_prev, from_next = look.at[pl.ds(BAND, HALO)], look.at[pl.ds(BAND + HALO, HALO)]
    halo_up = flow(1, r.halo_out, from_prev)
    halo_down = flow(2, r.halo_out, from_next)
    halo_up.send(r.halo_out, from_prev, next_band)
    halo_down.send(r.halo_out, from_next, prev_band)

    def project(i):
        rows = at(i, EB)
        block = look[rows, :]
        proj[rows, :] = dot(block, r.ew1[:L, :]).astype(BF16)
        proj[pl.ds(pl.multiple_of(LOOK + i * EB, EB), EB), :] = dot(block, r.ew1[L : 2 * L, :]).astype(BF16)

    loop(BAND // EB, project)

    def own_part(i):
        rows = at(i, ROWS)
        pre[rows, :] += dot(hot[rows, :BAND], proj[:BAND, :]) + dot(hot[rows, LOOK:], proj[LOOK:, :])

    loop(NBLK, own_part)
    halo_up.wait()
    halo_down.wait()
    proj[BAND:LOOK, :] = dot(look[BAND:, :], r.ew1[:L, :]).astype(BF16)

    hidden, normed, inv, msg = r.hidden, r.normed, r.inv, r.msg

    def edge_forward(i):
        rows = at(i, ROWS)
        pre_act = pre[rows, :] + dot(hot[rows, BAND:LOOK], proj[BAND:LOOK, :])
        sig = jax.nn.sigmoid(pre_act)
        hid = (pre_act * sig).astype(BF16)
        hidden[rows, :] = hid
        pre[rows, :] = sig * (1.0 + pre_act * (1.0 - sig))
        norm, inv_dev = layer_norm(dot(hid, r.ew2[...]) + r.eb2[...])
        normed[rows, :] = norm
        inv[rows, :] = inv_dev
        msg[rows, :] = (norm * r.live[rows, :]).astype(BF16)

    loop(NBLK, edge_forward)

    agg_out, agg_in = r.agg_out, r.agg_in

    def sum_messages(i):
        agg_out[at(i, EB), :] = dot(hot_t[pl.ds(pl.multiple_of(LOOK + i * EB, EB), EB), :], msg[...]).astype(BF16)

    loop(BAND // EB, sum_messages)
    agg_flow = flow(3, others, agg_in)
    for k in range(1, H):
        to = in_helper(k)
        agg_flow.send(agg_out.at[at(lax.rem(helper + k, H), N)], agg_in.at[pl.ds((k - 1) * N, N)], to)

    def hidden_turn(i):
        rows = at(i, ROWS)
        r.hidden_t[:, rows] = hidden[rows, :].T

    def look_turn(i):
        rows = at(i, EB)
        r.look_t[:, rows] = look[rows, :].T

    loop(NBLK, hidden_turn)
    loop(LOOK // EB, look_turn)
    agg_flow.wait()
    agg = agg_out[at(helper, N), :].astype(F32)
    for k in range(H - 1):
        agg += agg_in[k * N : (k + 1) * N, :].astype(F32)
    agg = agg.astype(BF16)

    node = r.node[...]
    nw1 = r.nw1
    n_pre = dot(node, nw1[:L, :]) + dot(agg, nw1[L:, :]) + r.nb1[...]
    n_sig = jax.nn.sigmoid(n_pre)
    n_hid = (n_pre * n_sig).astype(BF16)
    n_norm, n_inv = layer_norm(dot(n_hid, r.nw2[...]) + r.nb2[...])
    g_node = r.gnode[...].astype(F32)
    n_dz = norm_back(sea * g_node, n_norm, n_inv)
    n_dz_b = n_dz.astype(BF16)
    n_dpre = dot_nt(n_dz_b, r.nw2[...]) * (n_sig * (1.0 + n_pre * (1.0 - n_sig)))
    n_dpre_b = n_dpre.astype(BF16)
    agg_grad = r.agg_grad
    mine = agg_grad.at[at(helper, N)]
    agg_grad[at(helper, N), :] = dot_nt(n_dpre_b, nw1[L:, :]).astype(BF16)
    back_flow = flow(4, others, agg_grad.at[pl.ds(0, (H - 1) * N)])
    for k in range(1, H):
        back_flow.send(mine, mine, in_helper(k))

    own = (core * KINDS + kind_own) * (Y_HI * Y_LO) + y
    node_sums = Reduced(flows, r.n, dims, me, me, z_lo, z_hi, in_group, in_z_lo, in_z_hi)
    edge_sums = Reduced(flows, r.e, dims, me, own, z_lo, z_hi, in_group, in_z_lo, in_z_hi)

    bias_axes = (
        (r.bias0, H, helper, in_helper),
        (r.bias1, Y_HI * CORES, plane, in_plane),
        (r.bias2, Z_LO, z_lo, in_z_lo),
        (r.bias3, Z_HI, z_hi, in_z_hi),
    )

    def bias_send(step):
        ref, count, slot_i, device_of = bias_axes[step]
        mine = ref.at[slot_i]
        rest = ref.at[pl.ds(0, count - 1)]
        bias_flow = Flow(flows, r.bias_s.at[step], r.bias_r.at[step], rest, rest)
        for k in range(1, count):
            bias_flow.send(mine, mine, device_of(k))
        return bias_flow

    def bias_sum(step, bias_flow):
        ref, count = bias_axes[step][:2]
        bias_flow.wait()
        total = ref[0]
        for k in range(1, count):
            total += ref[k]
        return total

    node_sums.put(0, dot(node.T, n_dpre_b))
    node_sums.put(L, dot(agg.T, n_dpre_b))
    node_sums.put(2 * L, dot(n_hid.T, n_dz_b))
    node_sums.scatter()
    node_din = g_node + dot_nt(n_dpre_b, nw1[:L, :])

    load_grad.wait()
    gedge, dz_b, dpre_b = r.gedge, r.dz_b, r.dpre_b
    back_flow.wait()

    def edge_back(i, sums):
        rows = at(i, ROWS)
        grad = gedge[rows, :].astype(F32) + dot(hot[rows, LOOK:], agg_grad[...])
        dz = norm_back(grad * r.live[rows, :], normed[rows, :], inv[rows, :])
        second = dz.astype(BF16)
        dz_b[rows, :] = second
        dpre = dot_nt(second, r.ew2[...]) * pre[rows, :]
        dpre_b[rows, :] = dpre.astype(BF16)
        return sums[0] + jnp.sum(dpre, axis=0, keepdims=True), sums[1] + jnp.sum(dz, axis=0, keepdims=True)

    zero = jnp.zeros((1, L), F32)
    e_gb1, e_gb2 = lax.fori_loop(0, NBLK, edge_back, (zero, zero))

    scat = r.scat

    def scatter(i):
        rows = at(i, ROWS)
        scat[rows, :] = dot(hot_t[rows, :], dpre_b[...]).astype(BF16)

    edge_sums.put(3 * L, dot(r.hidden_t[...], dz_b[...]))
    edge_sums.scatter_kind(3, owner)
    edge_sums.put(2 * L, dot(r.edge_t[...], dpre_b[...]))
    edge_sums.scatter_kind(2, owner)
    loop(BAND // ROWS, lambda i: scatter(LOOK // ROWS + i))
    edge_sums.put(L, dot(r.look_t[:, :BAND], scat[LOOK:, :]))
    edge_sums.scatter_kind(1, owner)
    loop(LOOK // ROWS, scatter)
    edge_sums.put(0, dot(r.look_t[...], scat[:LOOK, :]))
    edge_sums.scatter_kind(0, owner)
    node_sums.along_z_lo()

    tiles = (e_gb1, e_gb2, jnp.sum(n_dpre, axis=0, keepdims=True), jnp.sum(n_dz, axis=0, keepdims=True))
    for i, row in enumerate(tiles):
        r.bias0[helper, 2 * i : 2 * i + 1, :] = row[:, :LANES]
        r.bias0[helper, 2 * i + 1 : 2 * i + 2, :] = row[:, LANES:]
    bias_flow = bias_send(0)

    halo_back, halo_in = r.halo_back, r.halo_in
    halo_back[...] = dot_nt(scat[BAND:LOOK, :], r.ew1[:L, :]).astype(BF16)
    upper, lower = pl.ds(0, HALO), pl.ds(HALO, HALO)
    back_down = flow(5, halo_back.at[upper], halo_in.at[upper])
    back_up = flow(6, halo_back.at[lower], halo_in.at[lower])
    back_down.send(halo_back.at[upper], halo_in.at[upper], prev_band)
    back_up.send(halo_back.at[lower], halo_in.at[lower], next_band)

    node_sums.along_z_hi()

    band_grad = r.band_grad
    band_grad[...] = dot_nt(scat[:BAND, :], r.ew1[:L, :]) + dot_nt(scat[LOOK:, :], r.ew1[L : 2 * L, :])

    r.bias1[plane] = bias_sum(0, bias_flow)
    bias_flow = bias_send(1)
    edge_sums.along_z_lo()

    node_sums.gather()

    r.bias2[z_lo] = bias_sum(1, bias_flow)
    bias_flow = bias_send(2)
    edge_sums.along_z_hi()

    back_down.wait()
    back_up.wait()
    node_out, node_in = r.node_out, r.node_in
    node_out[...] = (band_grad[...] + dot(r.halo_t[...], halo_in[...])).astype(BF16)
    node_flow = flow(7, others, node_in)
    for k in range(1, H):
        to = in_helper(k)
        node_flow.send(node_out.at[at(lax.rem(helper + k, H), N)], node_in.at[pl.ds((k - 1) * N, N)], to)

    def edge_grad(i):
        rows = at(i, ROWS)
        din = dot_nt(dpre_b[rows, :], r.ew1[2 * L :, :])
        r.edge_new[rows, :] = ((gedge[rows, :].astype(F32) + din) * r.live[rows, :]).astype(BF16)

    loop(NBLK, edge_grad)
    Local(flows, r.edge_new, r.o_edge, r.load_sem.at[2])

    r.bias3[z_hi] = bias_sum(2, bias_flow)
    bias_flow = bias_send(3)
    edge_sums.gather()

    node_flow.wait()
    total = node_out[at(helper, N), :].astype(F32)
    for k in range(H - 1):
        total += node_in[k * N : (k + 1) * N, :].astype(F32)
    r.o_node[...] = total + node_din
    r.o_bias[...] = bias_sum(3, bias_flow)
    node_sums.done.wait()
    edge_sums.done.wait()


class Reduced:
    def __init__(self, flows, refs, dims, me, own, z_lo, z_hi, in_group, in_z_lo, in_z_hi):
        self.flows, self.refs, self.me, self.own, self.z_lo, self.z_hi = flows, refs, me, own, z_lo, z_hi
        self.in_group, self.in_z_lo, self.in_z_hi = in_group, in_z_lo, in_z_hi
        self.G = dims.G
        self.piece = refs.out.shape[0] // dims.G
        rest = pl.ds(0, (self.G - 1) * self.piece)
        self.first = self.flow(0, refs.out.at[rest], refs.land.at[rest])

    def flow(self, i, sent, landed):
        return Flow(self.flows, self.refs.s.at[i], self.refs.r.at[i], sent, landed)

    def put(self, first, value):
        out = self.refs.out
        half, count = out.shape[0] // 2, value.shape[0]
        out[first : first + count, :] = value[:, :LANES].astype(BF16)
        out[half + first : half + first + count, :] = value[:, LANES:].astype(BF16)

    def scatter_to(self, g, piece_i, device):
        piece = self.piece
        self.first.send(self.refs.out.at[at(piece_i, piece)], self.refs.land.at[at(self.me, piece)], device)

    def scatter(self):
        for k in range(1, self.G):
            g, to = self.in_group(k)
            self.scatter_to(g, g, to)

    def scatter_kind(self, kind, owner):
        for j in range(self.G // 4):
            g, piece_i, to = owner(kind, j)

            @pl.when(g != self.me)
            def _():
                self.scatter_to(g, piece_i, to)

    def along_z_lo(self):
        out, land, quad, piece = self.refs.out, self.refs.land, self.refs.z_lo, self.piece
        self.first.wait()
        land[at(self.me, piece), :] = out[at(self.own, piece), :]
        zero = jnp.zeros((piece, LANES), F32)
        total = lax.fori_loop(0, self.G, lambda k, acc: acc + land[at(k, piece), :].astype(F32), zero)
        mine = quad.at[self.z_lo]
        quad[self.z_lo] = total.astype(BF16)
        rest = quad.at[pl.ds(0, Z_LO - 1)]
        self.second = self.flow(1, rest, rest)
        for k in range(1, Z_LO):
            self.second.send(mine, mine, self.in_z_lo(k))

    def along_z_hi(self):
        old, quad = self.refs.z_lo, self.refs.z_hi
        self.second.wait()
        total = old[0].astype(F32)
        for k in range(1, Z_LO):
            total += old[k].astype(F32)
        mine = quad.at[self.z_hi]
        quad[self.z_hi] = total.astype(BF16)
        rest = quad.at[pl.ds(0, Z_HI - 1)]
        self.third = self.flow(2, rest, rest)
        for k in range(1, Z_HI):
            self.third.send(mine, mine, self.in_z_hi(k))

    def gather(self):
        quad, full, piece = self.refs.z_hi, self.refs.full, self.piece
        self.third.wait()
        total = quad[0].astype(F32)
        for k in range(1, Z_HI):
            total += quad[k].astype(F32)
        mine = full.at[at(self.own, piece)]
        full[at(self.own, piece), :] = total.astype(BF16)
        rest = full.at[pl.ds(0, (self.G - 1) * piece)]
        self.done = self.flow(3, rest, rest)
        for k in range(1, self.G):
            self.done.send(mine, mine, self.in_group(k)[1])


def finish(dims, node_hbm, edge_hbm, node_sums_hbm, edge_sums_hbm, bias_hbm, o_node, o_edge, *rest):
    o_ew1, o_eb1, o_ew2, o_eb2, o_nw1, o_nb1, o_nw2, o_nb2, node_sums, edge_sums, bias, sems = rest
    pairs = (
        (edge_sums_hbm, edge_sums),
        (node_sums_hbm, node_sums),
        (bias_hbm, bias),
        (edge_hbm, o_edge),
        (node_hbm, o_node),
    )
    copies = [pltpu.make_async_copy(src, dst, sems.at[i]) for i, (src, dst) in enumerate(pairs)]
    for copy in copies:
        copy.start()

    def weights(full, targets, scale):
        half, first = full.shape[0] // 2, 0
        for out in targets:
            count = out.shape[0]
            out[:, :LANES] = full[first : first + count, :].astype(F32) * scale
            out[:, LANES:] = full[half + first : half + first + count, :].astype(F32) * scale
            first += count

    copies[0].wait()
    weights(edge_sums, (o_ew1, o_ew2), dims.edge_scale)
    copies[1].wait()
    weights(node_sums, (o_nw1, o_nw2), dims.node_scale)
    copies[2].wait()
    for i, (out, scale) in enumerate(
        ((o_eb1, dims.edge_scale), (o_eb2, dims.edge_scale), (o_nb1, dims.node_scale), (o_nb2, dims.node_scale))
    ):
        out[:, :LANES] = bias[2 * i : 2 * i + 1, :] * scale
        out[:, LANES:] = bias[2 * i + 1 : 2 * i + 2, :] * scale
    copies[3].wait()
    copies[4].wait()


def on_device(
    node_latent,
    edge_latent,
    grad_out_node,
    grad_out_edge,
    senders,
    receivers,
    band_edges,
    halo_list,
    sea_mask,
    edge_w1,
    edge_b1,
    edge_w2,
    edge_b2,
    node_w1,
    node_b1,
    node_w2,
    node_b2,
):
    H = lax.axis_size("helper")
    bands = lax.axis_size("band")
    N, L = node_latent.shape
    E = edge_latent.shape[0]
    HALO = halo_list.shape[1]
    BAND = N * H
    LOOK = BAND + 2 * HALO
    ALL = LOOK + BAND
    G = H * Y_HI * CORES
    dims = SimpleNamespace(
        H=H,
        E=E,
        N=N,
        HALO=HALO,
        L=L,
        G=G,
        edge_scale=1.0 / math.sqrt(E * H * bands),
        node_scale=1.0 / math.sqrt(N * H * bands),
    )
    V, S, ANY = pltpu.VMEM, pltpu.SMEM, pl.ANY
    inputs = dict(
        node=(node_latent, V),
        edge_hbm=(edge_latent, ANY),
        gnode=(grad_out_node, V),
        gedge_hbm=(grad_out_edge, ANY),
        send_ids=(senders.reshape(E // EB, EB), V),
        recv_ids=(receivers.reshape(E // EB, EB), V),
        band_edges=(band_edges, S),
        halo=(halo_list, V),
        sea=(sea_mask.reshape(1, N), V),
        ew1=(edge_w1, V),
        eb1=(edge_b1.reshape(1, L), V),
        ew2=(edge_w2, V),
        eb2=(edge_b2.reshape(1, L), V),
        nw1=(node_w1, V),
        nb1=(node_b1.reshape(1, L), V),
        nw2=(node_w2, V),
        nb2=(node_b2.reshape(1, L), V),
    )
    n_rows, e_rows = 3 * L * (L // LANES), 4 * L * (L // LANES)
    outputs = dict(
        o_node=((N, L), F32, V),
        o_edge=((E, L), BF16, ANY),
        n_full=((n_rows, LANES), BF16, V),
        e_full=((e_rows, LANES), BF16, V),
        o_bias=((8, LANES), F32, V),
    )
    scratch = dict(
        edge=V((E, L), BF16),
        gedge=V((E, L), BF16),
        edge_new=V((E, L), BF16),
        look=V((LOOK, L), BF16),
        look_t=V((L, LOOK), BF16),
        edge_t=V((L, E), BF16),
        hidden_t=V((L, E), BF16),
        proj=V((ALL, L), BF16),
        hot=V((E, ALL), BF16),
        hot_t=V((ALL, E), BF16),
        halo_t=V((BAND, 2 * HALO), BF16),
        halo_out=V((HALO, L), BF16),
        halo_back=V((2 * HALO, L), BF16),
        halo_in=V((2 * HALO, L), BF16),
        live=V((E, 1), F32),
        pre=V((E, L), F32),
        hidden=V((E, L), BF16),
        normed=V((E, L), F32),
        inv=V((E, 1), F32),
        msg=V((E, L), BF16),
        dz_b=V((E, L), BF16),
        dpre_b=V((E, L), BF16),
        agg_out=V((BAND, L), BF16),
        agg_in=V((BAND - N, L), BF16),
        agg_grad=V((BAND, L), BF16),
        scat=V((ALL, L), BF16),
        band_grad=V((BAND, L), F32),
        node_out=V((BAND, L), BF16),
        node_in=V((BAND - N, L), BF16),
        n_out=V((n_rows, LANES), BF16),
        n_land=V((n_rows, LANES), BF16),
        n_z_lo=V((Z_LO, n_rows // G, LANES), BF16),
        n_z_hi=V((Z_HI, n_rows // G, LANES), BF16),
        e_out=V((e_rows, LANES), BF16),
        e_land=V((e_rows, LANES), BF16),
        e_z_lo=V((Z_LO, e_rows // G, LANES), BF16),
        e_z_hi=V((Z_HI, e_rows // G, LANES), BF16),
        bias0=V((H, 8, LANES), F32),
        bias1=V((Y_HI * CORES, 8, LANES), F32),
        bias2=V((Z_LO, 8, LANES), F32),
        bias3=V((Z_HI, 8, LANES), F32),
    )
    DMA = pltpu.SemaphoreType.DMA
    scratch.update(load_sem=DMA((3,)), s_sem=DMA((8,)), r_sem=DMA((8,)), n_s=DMA((4,)), n_r=DMA((4,)))
    scratch.update(e_s=DMA((4,)), e_r=DMA((4,)), bias_s=DMA((4,)), bias_r=DMA((4,)))
    node, edge, node_sums, edge_sums, bias = pl.pallas_call(
        functools.partial(kernel, dims, list(inputs) + list(outputs) + list(scratch)),
        out_shape=[jax.ShapeDtypeStruct(shape, dtype) for shape, dtype, _ in outputs.values()],
        in_specs=[pl.BlockSpec(memory_space=space) for _, space in inputs.values()],
        out_specs=[pl.BlockSpec(memory_space=space) for _, _, space in outputs.values()],
        scratch_shapes=list(scratch.values()),
        compiler_params=pltpu.CompilerParams(
            collective_id=0, has_side_effects=True, vmem_limit_bytes=VMEM_BYTES
        ),
        name="layer_back",
    )(*[x for x, _ in inputs.values()])
    shapes = [(N, L), (E, L), (3 * L, L), (1, L), (L, L), (1, L), (2 * L, L), (1, L), (L, L), (1, L)]
    out = pl.pallas_call(
        functools.partial(finish, dims),
        out_shape=[jax.ShapeDtypeStruct(shape, BF16 if i == 1 else F32) for i, shape in enumerate(shapes)],
        in_specs=[pl.BlockSpec(memory_space=ANY)] * 5,
        out_specs=[pl.BlockSpec(memory_space=V)] * 10,
        scratch_shapes=[V((n_rows, LANES), BF16), V((e_rows, LANES), BF16), V((8, LANES), F32), DMA((5,))],
        compiler_params=pltpu.CompilerParams(vmem_limit_bytes=VMEM_BYTES),
        name="finish",
    )(node, edge, node_sums, edge_sums, bias)
    return tuple(x.reshape(L) if x.shape[0] == 1 else x for x in out)


def solution(mesh):
    rows = P(("band", "helper"), None)
    flat = P(("band", "helper"))
    in_specs = (rows,) * 4 + (flat, flat, P(), P("band", None), flat) + (P(),) * 8
    out_specs = (rows, rows) + (P(),) * 8
    return jax.shard_map(on_device, mesh=mesh, in_specs=in_specs, out_specs=out_specs, check_vma=False)
```

time: 894 us -> 80.6 us (0.09)
  waiting for transfers between devices: 488 us -> 0 us
  blocking collectives: 254 us -> 0 us
  Pallas kernels: 0 us -> 79.8 us
  starting transfers between devices: 74.2 us -> 0 us
  local copies, waits for them, and re-layouts: 24.3 us -> 0 us
  other arithmetic: 20.2 us -> 0 us
  between operations: 14.8 us -> 0.66 us
  matrix products: 9.32 us -> 0 us
    psum x1 -> x0, waiting for transfers between devices: 411 us -> none  [on_device(): lax.psum((edge_wgrads[0] * edge_scale, edge_wgrads[1] * edge_scale, edge_...]
    psum x1 -> x0, blocking collectives: 208 us -> none  [on_device(): lax.psum((edge_wgrads[0] * edge_scale, edge_wgrads[1] * edge_scale, edge_...]
    pallas_call x0 -> x2, Pallas kernels: none -> 79.8 us  [the longest x1 77 us: on_device(): pl.pallas_call(functools.partial(kernel, dims, list(inputs) + list(output...]
    reduce_scatter x2 -> x0, waiting for transfers between devices: 76.7 us -> none  [the longest x1 76.6 us: on_device(): lax.psum_scatter(agg_rows, 'helper', scatter_dimension=0, tiled=True)]
    ppermute x4 -> x0, starting transfers between devices: 74.1 us -> none  [passed_along(): lax.ppermute(array, axis, [(i, (i + by) % count) for i in range(count)])]
    all_gather x2 -> x0, blocking collectives: 45.8 us -> none  [the longest x1 23.7 us: on_device(): band_rows = lax.all_gather(node_latent, 'helper', axis=0, tiled=True)]
    unnamed x64 -> x0, local copies, waits for them, and re-layouts: 12.4 us -> none
    dot_general x15 -> x0, matrix products: 9.32 us -> none  [the longest x5 2.8 us: dot_left_t(): lax.dot_general(left_op, right_op, (((0,), (0,)), ((), ())), preferred_el...]
  transfers between devices with their start and end apart: 7 -> 0, of which waited for: 3 -> 0; matrix products, arithmetic and copies ran while one was open for 1% -> 0% of each run, Pallas kernels for 0% -> 0%
where the time goes in v1:
time: 80.6 us; the launch traced here: 80.5 us
  Pallas kernels  79.8 us (99%)
    pallas_call x1, Pallas kernels, on_device(): pl.pallas_call(functools.partial(kernel, dims, list(inputs) + list(output...  77 us
    pallas_call x1, Pallas kernels, on_device(): pl.pallas_call(functools.partial(finish, dims), out_shape=[jax.ShapeDtype...  2.8 us

profile of v1, /device:TPU:1, one launch (start us, length us, event | category | flops | bytes accessed | tf_op | source)
XLA Modules:
  0.0 80.5 jit_solution(10339498929487707975)
XLA Ops:
  0.6 77.0 %layer_back.1 = (f32[64,256]{1,0:T(8,128)}, bf16[1024,256]{1,0:T(8,128)(2,1)}, bf16[1536,128]{1,0:T(8,128)(2,1)}, bf16[2048,128]{1,0:T(8,128)(2,1)}, f32[8,128]{1,0:T(8,128)}) custom-call(bf16[64,256]{1,0:T(8,128)(2,1)} %refs_0_.1, bf16[1024,256]{1,0:T(8,128)(2,1)} %refs_1_.1, bf16[64,256]{1,0:T(8,128)(2,1)} %refs_2_.1, bf16[1024,256]{1,0:T(8,128)(2,1)} %refs_3_.1, ...), custom_call_target="tpu_custom_call" | custom-call | tf_op jit(solution)/shard_map/layer_back/pallas_call | solution.py:690
  77.7 2.8 %finish.1 = (f32[64,256]{1,0:T(8,128)}, bf16[1024,256]{1,0:T(8,128)(2,1)}, f32[768,256]{1,0:T(8,128)}, f32[1,256]{1,0:T(1,128)}, f32[256,256]{1,0:T(8,128)}, /*i...) custom-call(f32[64,256]{1,0:T(8,128)} %get-tuple-element.25.node_hbm, ...), custom_call_target="tpu_custom_call" | custom-call | tf_op jit(solution)/shard_map/finish/pallas_call | solution.py:702

commit v2 on v1

--- a/solution.py
+++ b/solution.py
@@ -172,6 +172,10 @@
     def in_group(k):
         g = lax.rem(me + k, G)
         return g, place(lax.div(g, H), z, lax.rem(g, H))
+
+    def in_core(k):
+        t = lax.rem(y_hi * H + helper + k, Y_HI * H)
+        return place(lax.div(t, H) * CORES + core, z, lax.rem(t, H))
 
     def in_helper(k):
         return dict(band=band, helper=lax.rem(helper + k, H))
@@ -337,8 +341,8 @@
         back_flow.send(mine, mine, in_helper(k))
 
     own = (core * KINDS + kind_own) * (Y_HI * Y_LO) + y
-    node_sums = Reduced(flows, r.n, dims, me, me, z_lo, z_hi, in_group, in_z_lo, in_z_hi)
-    edge_sums = Reduced(flows, r.e, dims, me, own, z_lo, z_hi, in_group, in_z_lo, in_z_hi)
+    node_sums = Reduced(flows, r.n, dims, me, me, z_lo, z_hi, in_group, in_core, in_z_lo, in_z_hi)
+    edge_sums = Reduced(flows, r.e, dims, me, own, z_lo, z_hi, in_group, in_core, in_z_lo, in_z_hi)
 
     bias_axes = (
         (r.bias0, H, helper, in_helper),
@@ -428,12 +432,6 @@
     bias_flow = bias_send(1)
     edge_sums.along_z_lo()
 
-    node_sums.gather()
-
-    r.bias2[z_lo] = bias_sum(1, bias_flow)
-    bias_flow = bias_send(2)
-    edge_sums.along_z_hi()
-
     back_down.wait()
     back_up.wait()
     node_out, node_in = r.node_out, r.node_in
@@ -443,6 +441,12 @@
         to = in_helper(k)
         node_flow.send(node_out.at[at(lax.rem(helper + k, H), N)], node_in.at[pl.ds((k - 1) * N, N)], to)
 
+    r.bias2[z_lo] = bias_sum(1, bias_flow)
+    bias_flow = bias_send(2)
+    edge_sums.along_z_hi()
+
+    node_sums.gather()
+
     def edge_grad(i):
         rows = at(i, ROWS)
         din = dot_nt(dpre_b[rows, :], r.ew1[2 * L :, :])
@@ -455,20 +459,23 @@
     bias_flow = bias_send(3)
     edge_sums.gather()
 
+    mate = place(y_hi * CORES + 1 - core, z, helper)
+    node_sums.hand_on(mate, [(i * CORES + core) * H for i in range(Y_HI)])
     node_flow.wait()
     total = node_out[at(helper, N), :].astype(F32)
     for k in range(H - 1):
         total += node_in[k * N : (k + 1) * N, :].astype(F32)
     r.o_node[...] = total + node_din
     r.o_bias[...] = bias_sum(3, bias_flow)
-    node_sums.done.wait()
-    edge_sums.done.wait()
+    edge_sums.hand_on(mate, [core * (G // CORES)])
+    node_sums.handed.wait()
+    edge_sums.handed.wait()
 
 
 class Reduced:
-    def __init__(self, flows, refs, dims, me, own, z_lo, z_hi, in_group, in_z_lo, in_z_hi):
+    def __init__(self, flows, refs, dims, me, own, z_lo, z_hi, in_group, in_core, in_z_lo, in_z_hi):
         self.flows, self.refs, self.me, self.own, self.z_lo, self.z_hi = flows, refs, me, own, z_lo, z_hi
-        self.in_group, self.in_z_lo, self.in_z_hi = in_group, in_z_lo, in_z_hi
+        self.in_group, self.in_core, self.in_z_lo, self.in_z_hi = in_group, in_core, in_z_lo, in_z_hi
         self.G = dims.G
         self.piece = refs.out.shape[0] // dims.G
         rest = pl.ds(0, (self.G - 1) * self.piece)
@@ -527,17 +534,27 @@
             self.third.send(mine, mine, self.in_z_hi(k))
 
     def gather(self):
-        quad, full, piece = self.refs.z_hi, self.refs.full, self.piece
+        quad, full, piece, half = self.refs.z_hi, self.refs.full, self.piece, self.G // 2
         self.third.wait()
         total = quad[0].astype(F32)
         for k in range(1, Z_HI):
             total += quad[k].astype(F32)
         mine = full.at[at(self.own, piece)]
         full[at(self.own, piece), :] = total.astype(BF16)
-        rest = full.at[pl.ds(0, (self.G - 1) * piece)]
+        rest = full.at[pl.ds(0, (half - 1) * piece)]
         self.done = self.flow(3, rest, rest)
-        for k in range(1, self.G):
-            self.done.send(mine, mine, self.in_group(k)[1])
+        for k in range(1, half):
+            self.done.send(mine, mine, self.in_core(k))
+
+    def hand_on(self, mate, firsts):
+        full, half = self.refs.full, self.G // 2
+        self.done.wait()
+        whole = full.at[pl.ds(0, half * self.piece)]
+        self.handed = self.flow(4, whole, whole)
+        count = half * self.piece // len(firsts)
+        for first in firsts:
+            part = full.at[pl.ds(pl.multiple_of(first * self.piece, 16), count)]
+            self.handed.send(part, part, mate)
 
 
 def finish(dims, node_hbm, edge_hbm, node_sums_hbm, edge_sums_hbm, bias_hbm, o_node, o_edge, *rest):
@@ -685,8 +702,8 @@
         bias3=V((Z_HI, 8, LANES), F32),
     )
     DMA = pltpu.SemaphoreType.DMA
-    scratch.update(load_sem=DMA((3,)), s_sem=DMA((8,)), r_sem=DMA((8,)), n_s=DMA((4,)), n_r=DMA((4,)))
-    scratch.update(e_s=DMA((4,)), e_r=DMA((4,)), bias_s=DMA((4,)), bias_r=DMA((4,)))
+    scratch.update(load_sem=DMA((3,)), s_sem=DMA((8,)), r_sem=DMA((8,)), n_s=DMA((5,)), n_r=DMA((5,)))
+    scratch.update(e_s=DMA((5,)), e_r=DMA((5,)), bias_s=DMA((4,)), bias_r=DMA((4,)))
     node, edge, node_sums, edge_sums, bias = pl.pallas_call(
         functools.partial(kernel, dims, list(inputs) + list(outputs) + list(scratch)),
         out_shape=[jax.ShapeDtypeStruct(shape, dtype) for shape, dtype, _ in outputs.values()],

time: 80.6 us -> 77.3 us (0.959)
  Pallas kernels: 79.8 us -> 76.4 us
    pallas_call x1, Pallas kernels: 77 us -> 73.6 us  [on_device(): pl.pallas_call(functools.partial(kernel, dims, list(inputs) + list(output...]
where the time goes in v2:
time: 77.3 us; the launch traced here: 77.1 us
  Pallas kernels  76.4 us (99%)
    pallas_call x1, Pallas kernels, on_device(): pl.pallas_call(functools.partial(kernel, dims, list(inputs) + list(output...  73.6 us
    pallas_call x1, Pallas kernels, on_device(): pl.pallas_call(functools.partial(finish, dims), out_shape=[jax.ShapeDtype...  2.8 us

profile of v2, /device:TPU:1, one launch (start us, length us, event | category | flops | bytes accessed | tf_op | source)
XLA Modules:
  0.0 77.1 jit_solution(8458295530503005877)
XLA Ops:
  0.6 73.6 %layer_back.1 = (f32[64,256]{1,0:T(8,128)}, bf16[1024,256]{1,0:T(8,128)(2,1)}, bf16[1536,128]{1,0:T(8,128)(2,1)}, bf16[2048,128]{1,0:T(8,128)(2,1)}, f32[8,128]{1,0:T(8,128)}) custom-call(bf16[64,256]{1,0:T(8,128)(2,1)} %refs_0_.1, bf16[1024,256]{1,0:T(8,128)(2,1)} %refs_1_.1, bf16[64,256]{1,0:T(8,128)(2,1)} %refs_2_.1, bf16[1024,256]{1,0:T(8,128)(2,1)} %refs_3_.1, ...), custom_call_target="tpu_custom_call" | custom-call | tf_op jit(solution)/shard_map/layer_back/pallas_call | solution.py:707
  74.3 2.8 %finish.1 = (f32[64,256]{1,0:T(8,128)}, bf16[1024,256]{1,0:T(8,128)(2,1)}, f32[768,256]{1,0:T(8,128)}, f32[1,256]{1,0:T(1,128)}, f32[256,256]{1,0:T(8,128)}, /*i...) custom-call(f32[64,256]{1,0:T(8,128)} %get-tuple-element.25.node_hbm, ...), custom_call_target="tpu_custom_call" | custom-call | tf_op jit(solution)/shard_map/finish/pallas_call | solution.py:719

commit v3 on v2

--- a/solution.py
+++ b/solution.py
@@ -196,6 +196,10 @@
         return Flow(flows, r.s_sem.at[i], r.r_sem.at[i], sent, landed)
 
     load_edge = Local(flows, r.edge_hbm, r.edge, r.load_sem.at[0])
+    load_ew1 = Local(flows, r.ew1_hbm, r.ew1, r.load_sem.at[3])
+    load_ew2 = Local(flows, r.ew2_hbm, r.ew2, r.load_sem.at[4])
+    load_nw1 = Local(flows, r.nw1_hbm, r.nw1, r.load_sem.at[5])
+    load_nw2 = Local(flows, r.nw2_hbm, r.nw2, r.load_sem.at[6])
     load_grad = Local(flows, r.gedge_hbm, r.gedge, r.load_sem.at[1])
 
     barrier = pltpu.get_barrier_semaphore()
@@ -244,6 +248,10 @@
     r.live[...] = jnp.where(slot * H + helper < live_blocks, 1.0, 0.0)
 
     load_edge.wait()
+    load_ew1.wait()
+    load_ew2.wait()
+    load_nw1.wait()
+    load_nw2.wait()
     edge, pre = r.edge, r.pre
 
     def edge_part(i):
@@ -641,13 +649,13 @@
         band_edges=(band_edges, S),
         halo=(halo_list, V),
         sea=(sea_mask.reshape(1, N), V),
-        ew1=(edge_w1, V),
+        ew1_hbm=(edge_w1, ANY),
         eb1=(edge_b1.reshape(1, L), V),
-        ew2=(edge_w2, V),
+        ew2_hbm=(edge_w2, ANY),
         eb2=(edge_b2.reshape(1, L), V),
-        nw1=(node_w1, V),
+        nw1_hbm=(node_w1, ANY),
         nb1=(node_b1.reshape(1, L), V),
-        nw2=(node_w2, V),
+        nw2_hbm=(node_w2, ANY),
         nb2=(node_b2.reshape(1, L), V),
     )
     n_rows, e_rows = 3 * L * (L // LANES), 4 * L * (L // LANES)
@@ -660,6 +668,10 @@
     )
     scratch = dict(
         edge=V((E, L), BF16),
+        ew1=V((3 * L, L), BF16),
+        ew2=V((L, L), BF16),
+        nw1=V((2 * L, L), BF16),
+        nw2=V((L, L), BF16),
         gedge=V((E, L), BF16),
         edge_new=V((E, L), BF16),
         look=V((LOOK, L), BF16),
@@ -702,7 +714,7 @@
         bias3=V((Z_HI, 8, LANES), F32),
     )
     DMA = pltpu.SemaphoreType.DMA
-    scratch.update(load_sem=DMA((3,)), s_sem=DMA((8,)), r_sem=DMA((8,)), n_s=DMA((5,)), n_r=DMA((5,)))
+    scratch.update(load_sem=DMA((7,)), s_sem=DMA((8,)), r_sem=DMA((8,)), n_s=DMA((5,)), n_r=DMA((5,)))
     scratch.update(e_s=DMA((5,)), e_r=DMA((5,)), bias_s=DMA((4,)), bias_r=DMA((4,)))
     node, edge, node_sums, edge_sums, bias = pl.pallas_call(
         functools.partial(kernel, dims, list(inputs) + list(outputs) + list(scratch)),

time: 77.3 us -> 76.9 us (level)
  no operation moved by 1% of the time
where the time goes in v3:
time: 76.9 us; the launch traced here: 76.7 us
  Pallas kernels  76 us (99%)
    pallas_call x1, Pallas kernels, on_device(): pl.pallas_call(functools.partial(kernel, dims, list(inputs) + list(output...  73.2 us
    pallas_call x1, Pallas kernels, on_device(): pl.pallas_call(functools.partial(finish, dims), out_shape=[jax.ShapeDtype...  2.8 us

profile of v3, /device:TPU:1, one launch (start us, length us, event | category | flops | bytes accessed | tf_op | source)
XLA Modules:
  0.0 76.7 jit_solution(15836593322198712163)
XLA Ops:
  0.6 73.2 %layer_back.1 = (f32[64,256]{1,0:T(8,128)}, bf16[1024,256]{1,0:T(8,128)(2,1)}, bf16[1536,128]{1,0:T(8,128)(2,1)}, bf16[2048,128]{1,0:T(8,128)(2,1)}, f32[8,128]{1,0:T(8,128)}) custom-call(bf16[64,256]{1,0:T(8,128)(2,1)} %refs_0_.1, bf16[1024,256]{1,0:T(8,128)(2,1)} %refs_1_.1, bf16[64,256]{1,0:T(8,128)(2,1)} %refs_2_.1, bf16[1024,256]{1,0:T(8,128)(2,1)} %refs_3_.1, ...), custom_call_target="tpu_custom_call" | custom-call | tf_op jit(solution)/shard_map/layer_back/pallas_call | solution.py:719
  73.9 2.8 %finish.1 = (f32[64,256]{1,0:T(8,128)}, bf16[1024,256]{1,0:T(8,128)(2,1)}, f32[768,256]{1,0:T(8,128)}, f32[1,256]{1,0:T(1,128)}, f32[256,256]{1,0:T(8,128)}, /*i...) custom-call(f32[64,256]{1,0:T(8,128)} %get-tuple-element.25.node_hbm, ...), custom_call_target="tpu_custom_call" | custom-call | tf_op jit(solution)/shard_map/finish/pallas_call | solution.py:731
